TPU v7x, 128 devices: a whole 4x4x4 slice. The times are simulated.
128 devices in a mesh: feat: 8 (over x, core), rows: 16 (over z, y).
Axes of the slice: x: 4, y: 4, z: 4, core: 2. Of those that a mesh axis runs over, the one named last changes fastest.
Arguments:
- features: bfloat16 [128, 128, 768], P('feat', None, 'rows'), may hold values from -6 to 6
- w_in: bfloat16 [128, 256], replicated, may hold values from -0.5 to 0.5
- bias: float32 [256], replicated, may hold values from -4 to 4
- tiles: bfloat16 [768, 8, 128, 128], P(('feat', 'rows')), may hold values from 0 to 1, as said below
- tile_cols: int32 [768, 8], P(('feat', 'rows')), may hold values from 0 to 767, as said below
- tile_counts: int32 [768], P(('feat', 'rows')), may hold values from 1 to 8, as said below
- cotangent: bfloat16 [98304, 256], P(('feat', 'rows')), may hold values from -6 to 6
Outputs:
- hidden: bfloat16 [98304, 256], P(('feat', 'rows'))
- weight_grad: float32 [128, 256], P('feat')
Inputs may be any that keep to these rules, and one draw needn't show every extreme that they name: Each block row's count lies between 1 and 8; in every draw some device owns a block row with 8 live slots. Slots k >= tile_counts[I] are ignored. `tile_cols`: block row I on the device owning blocks s * 6 to s * 6 + 6 - 1 (s = I // 6) names column blocks J with J // 96 = I // 96 and (J - (s % 16) * 6 + 2) mod 96 below 10: its own blocks or up to 2 blocks of the neighbouring devices in its cycle, wrapping; both ends are reached. `tiles`: entries are 0 or 1.
All inputs are finite; a program needn't handle non-finite values.
Results may differ from a plain program's by a relative error of at most 0.008.
Values may be sent and summed in bfloat16 or wider, within the bound.
No kernel may reach another device: no remote copies, remote signals or barrier semaphores. Data moves between devices by JAX's collectives and lax.ppermute only.
A program may use at most 64 MiB of HBM per device.

v0:
```python
import jax
import jax.numpy as jnp
from jax import lax
from jax.sharding import PartitionSpec as P

HALO_BLK = 2


def padded(cells, sides, width):
    for axis, dim in sides:
        count = lax.axis_size(axis)
        head = lax.slice_in_dim(cells, 0, width, axis=dim)
        tail = lax.slice_in_dim(cells, cells.shape[dim] - width, cells.shape[dim], axis=dim)
        cells = jnp.concatenate(
            [
                lax.ppermute(tail, axis, [(i, (i + 1) % count) for i in range(count)]),
                cells,
                lax.ppermute(head, axis, [((i + 1) % count, i) for i in range(count)]),
            ],
            axis=dim,
        )
    return cells


def shifted(block, axis, distance):
    devices = range(lax.axis_size(axis))
    route = [((i - distance) % len(devices), i) for i in devices]
    return lax.ppermute(block, axis, route)


def gelu_parts(values):
    inner = 0.7978845608 * (values + 0.044715 * values * values * values)
    tangent = jnp.tanh(inner)
    output = 0.5 * values * (1.0 + tangent)
    slope = 0.5 * (1.0 + tangent) + 0.5 * values * (1.0 - tangent * tangent) * 0.7978845608 * (
        1.0 + 3.0 * 0.044715 * values * values
    )
    return (output, slope)


def halo_projected(projected, margin):
    return padded(projected, (("rows", 0),), margin)


def body(features, w_in, bias, tiles, tile_cols, tile_counts, cotangent):
    block_rows, slot_count, tile_side, unused_side = tiles.shape
    hidden_width = w_in.shape[1]
    feat_size = lax.axis_size("feat")
    row_size = lax.axis_size("rows")
    slice_width = w_in.shape[0] // feat_size
    nodes_dev = block_rows * tile_side
    sub_rows = nodes_dev // row_size
    feat_id = lax.axis_index("feat")
    row_id = lax.axis_index("rows")
    margin = HALO_BLK * tile_side
    w_own = lax.dynamic_slice_in_dim(w_in, feat_id * slice_width, slice_width, 0)
    partial_value = jnp.einsum(
        "cdn,ch->dnh", features, w_own, preferred_element_type=jnp.float32
    ).astype(jnp.bfloat16)
    received = lax.all_to_all(
        partial_value, ("feat", "rows"), split_axis=0, concat_axis=0, tiled=True
    )
    received = received.reshape(feat_size, nodes_dev, hidden_width)
    projected = jnp.sum(received.astype(jnp.float32), axis=0).astype(jnp.bfloat16)
    extended = halo_projected(projected, margin)
    ext_count = block_rows + 2 * HALO_BLK
    ext_blocks = extended.reshape(ext_count, tile_side, hidden_width)
    cycle_size = block_rows * row_size
    local_cols = (tile_cols - feat_id * cycle_size - row_id * block_rows + HALO_BLK) % cycle_size
    slot_ids = jnp.arange(slot_count, dtype=jnp.int32)
    live_slot = (slot_ids[None, :] < tile_counts[:, None]).astype(jnp.bfloat16)
    masked = tiles * live_slot[:, :, None, None]
    degree = jnp.sum(masked, axis=(1, 3), dtype=jnp.float32)
    neighbours = ext_blocks[local_cols]
    summed_rows = jnp.einsum(
        "bkij,bkjh->bih", masked, neighbours, preferred_element_type=jnp.float32
    )
    own_rows = projected.reshape(block_rows, tile_side, hidden_width).astype(jnp.float32)
    pre_act = (own_rows + summed_rows) / (degree[:, :, None] + 1.0) + bias
    activated, slope = gelu_parts(pre_act)
    hidden = activated.astype(jnp.bfloat16).reshape(nodes_dev, hidden_width)
    scaled = (
        cotangent.reshape(block_rows, tile_side, hidden_width).astype(jnp.float32)
        * slope
        / (degree[:, :, None] + 1.0)
    ).astype(jnp.bfloat16)
    targets = jnp.arange(ext_count, dtype=jnp.int32)
    onehot = (local_cols[:, :, None] == targets[None, None, :]).astype(jnp.bfloat16)
    combined = jnp.einsum(
        "bkq,bkij->qbij", onehot, masked, preferred_element_type=jnp.float32
    ).astype(jnp.bfloat16)
    ext_sums = jnp.einsum("qbij,bih->qjh", combined, scaled, preferred_element_type=jnp.float32)
    from_before = shifted(ext_sums[block_rows + HALO_BLK :].astype(jnp.bfloat16), "rows", 1).astype(
        jnp.float32
    )
    from_after = shifted(ext_sums[:HALO_BLK].astype(jnp.bfloat16), "rows", -1).astype(jnp.float32)
    own_sums = ext_sums[HALO_BLK : HALO_BLK + block_rows] + scaled.astype(jnp.float32)
    own_sums = own_sums.at[:HALO_BLK].add(from_before)
    own_sums = own_sums.at[block_rows - HALO_BLK :].add(from_after)
    grad_proj = own_sums.astype(jnp.bfloat16).reshape(nodes_dev, hidden_width)
    pieces = lax.all_to_all(
        grad_proj.reshape(row_size, sub_rows, hidden_width),
        "rows",
        split_axis=0,
        concat_axis=0,
        tiled=True,
    )
    grad_slice = jnp.einsum(
        "cdn,dnh->ch",
        features,
        lax.all_gather(pieces, "feat", axis=0, tiled=True),
        preferred_element_type=jnp.float32,
    )
    weight_grad = lax.psum(grad_slice, "rows")
    return (hidden, weight_grad)


def solution(mesh):
    in_specs = (
        P("feat", None, "rows"),
        P(),
        P(),
        P(("feat", "rows"), None, None, None),
        P(("feat", "rows"), None),
        P(("feat", "rows")),
        P(("feat", "rows"), None),
    )
    out_specs = (P(("feat", "rows"), None), P("feat", None))
    return jax.shard_map(body, mesh=mesh, in_specs=in_specs, out_specs=out_specs, check_vma=False)
```

profile of v0, /device:TPU:0, one launch (start us, length us, event | category | flops | bytes accessed | tf_op | source)
XLA Modules:
  0.0 216.6 jit_solution(2524314712389904341)
XLA Ops:
  7.2 0.0 copy-start
  7.2 0.8 copy-done
  8.0 1.9 convert_bitcast_fusion.1
  9.9 3.2 %copy.17 = bf16[128,48,256]{2,1,0:T(8,128)(2,1)} copy(bf16[128,48,256]{0,2,1:T(8,128)(2,1)S(1)} %convert_bitcast_fusion.1) | data formatting | bytes 6291456 | tf_op jit(solution)/shard_map/convert_element_type | solution.py:59
  13.1 0.0 copy-start.9
  13.1 0.0 copy-start.8
  13.1 11.1 %all-to-all-start = ((bf16[128,48,256]{2,1,0:T(8,128)(2,1)}), bf16[128,48,256]{2,1,0:T(8,128)(2,1)S(1)}, u32[]{:S(2)}, u32[]{:S(2)}) async-start(bf16[128,48,256]{2,1,0:T(8,128)(2,1)} %copy.17), calls=%async_computation | async-start | bytes 6291456 | tf_op jit(solution)/shard_map/all_to_all | solution.py:60
  24.3 0.0 all-gather.2.cloned.1.call-start
  24.3 0.0 copy-done.9
  24.3 0.1 fusion.27
  24.4 0.0 copy-done.8
  24.4 2.0 convert_reduce_fusion
  26.5 0.0 copy-start.1
  26.5 1.1 copy-done.1
  27.6 3.1 %convert_bitcast_fusion = bf16[10,6,128,128]{3,0,2,1:T(8,128)(2,1)} fusion(bf16[6,8,128,128]{3,2,1,0:T(8,128)(2,1)S(1)} %get-tuple-element.27, s32[6,8]{1,0:T(8,128)S(1)} %get-tuple-element.29), kind=kOutput, calls=%fused_computation.2 | convolution fusion | flops 16712160 | bytes 3539136 | tf_op jit(solution)/shard_map/bkq,bkij->qbij/dot_general | solution.py:89
  30.7 33.8 %all-to-all-done = bf16[128,48,256]{2,1,0:T(8,128)(2,1)S(1)} async-done(((bf16[128,48,256]{2,1,0:T(8,128)(2,1)}), bf16[128,48,256]{2,1,0:T(8,128)(2,1)S(1)}, u32[]{:S(2)}, u32[]{:S(2)}) %all-to-all-start) | async-done | bytes 3145760 | tf_op jit(solution)/shard_map/all_to_all | solution.py:60
  64.5 0.4 bitcast_reduce_fusion
  64.9 0.0 copy-start.4
  65.0 0.7 copy-done.4
  65.7 0.7 collective-permute-start
  66.4 4.7 %collective-permute-start.1 = (bf16[256,256]{1,0:T(8,128)(2,1)S(1)}, bf16[256,256]{1,0:T(8,128)(2,1)S(1)}, u32[]{:S(2)}, u32[]{:S(2)}) collective-permute-start(bf16[256,256]{1,0:T(8,128)(2,1)S(1)} %get-tuple-element.35), channel_id=1, source_target_pairs={{1,0},{2,1},{3,2},{4,3},{5,4},{6,5},{7,6},{8,7},{9,8},{10,9},{11,1... | collective-permute-start | bytes 393224 | tf_op jit(solution)/shard_map/ppermute | solution.py:18
  71.1 0.1 reshape.114
  71.2 2.9 %collective-permute-done = bf16[256,256]{1,0:T(8,128)(2,1)S(1)} collective-permute-done((bf16[256,256]{1,0:T(8,128)(2,1)S(1)}, bf16[256,256]{1,0:T(8,128)(2,1)S(1)}, u32[]{:S(2)}, u32[]{:S(2)}) %collective-permute-start) | collective-permute-done | bytes 131104 | tf_op jit(solution)/shard_map/ppermute | solution.py:16
  74.1 0.0 collective-permute-done.1
  74.1 1.0 pad_maximum_fusion
  75.1 0.0 copy-start.2
  75.1 0.0 copy-start.5
  75.1 0.0 copy-start.10
  75.2 2.5 %gather_fusion = bf16[48,128,256]{2,1,0:T(8,128)(2,1)} fusion(bf16[10,128,256]{2,1,0:T(8,128)(2,1)S(1)} %bitcast.47, s32[1024]{0:T(1024)S(1)} %pad_clamp_fusion), kind=kCustom, calls=%fused_computation | custom fusion | bytes 6291648 | tf_op jit(solution)/shard_map/gather | solution.py:74
  77.7 0.0 copy-done.2
  77.7 0.0 copy-done.5
  77.7 0.0 copy-done.10
  77.7 0.0 copy-start.3
  77.7 0.0 copy-start.7
  77.7 2.8 %fusion.8 = f32[6,128,256]{2,1,0:T(8,128)S(1)} fusion(bf16[6,8,128,128]{3,2,1,0:T(8,128)(2,1)S(1)} %copy-done.2, bf16[6,8,128,256]{3,2,1,0:T(8,128)(2,1)} %bitcast.49, bf16[6,128,256]{2,1,0:T(8,128)(2,1)S(1)} %bitcast.50, f32[256]{0:T(256)S(1)} %copy-done.10, f32[6,128]{1,0:T(8,128)S(1)} %broadcast_add_fusion), kind=kOutput, calls=%fused_computation.12 | convolution fusion | flops 403439616 | bytes 5902336 | tf_op jit(solution)/shard_map/bkij,bkjh->bih/dot_general | solution.py:75
  80.5 0.0 copy-done.3
  80.5 0.1 copy-done.7
  80.6 1.5 fusion.32
  82.1 0.1 collective-permute-start.2
  82.2 0.0 copy-start.6
  82.2 1.4 slice_add_fusion
  83.6 5.3 %collective-permute-start.3 = (bf16[2,128,256]{2,1,0:T(8,128)(2,1)S(1)}, bf16[2,128,256]{2,1,0:T(8,128)(2,1)S(1)}, u32[]{:S(2)}, u32[]{:S(2)}) collective-permute-start(bf16[2,128,256]{2,1,0:T(8,128)(2,1)S(1)} %get-tuple-element.32), channel_id=1, source_target_pairs={{1,0},{2,1},{3,2},{4,3},{5,4},{6,5},{7,6},{8,7},{9,8},{10,9},{11,1... | collective-permute-start | bytes 393224 | tf_op jit(solution)/shard_map/ppermute | solution.py:28
  88.9 1.6 collective-permute-done.2
  90.5 0.1 fusion.19
  90.5 0.9 collective-permute-done.3
  91.4 0.1 fusion.18
  91.5 16.3 %all_to_all.10 = bf16[16,48,256]{2,1,0:T(8,128)(2,1)S(1)} all-to-all(bf16[16,48,256]{2,1,0:T(8,128)(2,1)S(1)} %bitcast.51), channel_id=1, replica_groups=mesh['feat'=8,'rows'=16] {'rows'}, dimensions={0} | all-to-all | bytes 786432 | tf_op jit(solution)/shard_map/all_to_all | solution.py:101
  107.9 0.9 copy.20
  108.8 0.0 all-gather.2.cloned.1.call-update
  108.8 24.0 %all-gather.2.cloned.1.call-done = bf16[128,48,256]{2,0,1:T(8,128)(2,1)} async-done(((bf16[16,48,256]{2,0,1:T(8,128)(2,1)}), bf16[128,48,256]{2,0,1:T(8,128)(2,1)}) %all-gather.2.cloned.1.call-update) | async-done | bytes 3145744 | tf_op jit(solution)/shard_map/all_gather | solution.py:111
  132.8 0.0 copy-done.6
  132.8 2.4 %convolution_bitcast_fusion.1 = f32[16,256]{1,0:T(8,128)S(1)} fusion(bf16[128,48,256]{2,0,1:T(8,128)(2,1)} %all-gather.2.cloned.1.call-done, bf16[16,128,48]{1,2,0:T(8,128)(2,1)S(1)} %copy-done.6), kind=kOutput, calls=%fused_computation.15 | convolution fusion | flops 50331648 | bytes 3358720 | tf_op jit(solution)/shard_map/cdn,dnh->ch/dot_general | solution.py:108
  135.2 74.5 %psum.7 = f32[16,256]{1,0:T(8,128)} all-reduce(f32[16,256]{1,0:T(8,128)S(1)} %convolution_bitcast_fusion.1), channel_id=1, replica_groups=mesh['feat'=8,'rows'=16] {'rows'}, use_global_device_ids=true, to_apply=%region_2.3 | all-reduce | flops 4096 | bytes 32768 | tf_op jit(solution)/shard_map/psum | solution.py:114
  (6 shorter events, 0.1 us)
Async XLA Ops:
  7.2 0.8 copy-start
  13.1 11.2 %copy-start.9 = (s32[6]{0:T(128)S(1)}, s32[6]{0:T(128)}, u32[]{:S(2)}) copy-start(s32[6]{0:T(128)} %param.16) | copy-start | bytes 76
  13.1 11.3 %copy-start.8 = (s32[6,8]{1,0:T(8,128)S(1)}, s32[6,8]{1,0:T(8,128)}, u32[]{:S(2)}) copy-start(s32[6,8]{1,0:T(8,128)} %param.15) | copy-start | bytes 580
  13.1 51.4 %all-to-all-start = ((bf16[128,48,256]{2,1,0:T(8,128)(2,1)}), bf16[128,48,256]{2,1,0:T(8,128)(2,1)S(1)}, u32[]{:S(2)}, u32[]{:S(2)}) async-start(bf16[128,48,256]{2,1,0:T(8,128)(2,1)} %copy.17), calls=%async_computation | async-start | bytes 6291456 | tf_op jit(solution)/shard_map/all_to_all | solution.py:60
  24.3 108.5 %all-gather.2.cloned.1.call-start = ((), (), s32[]{:S(2)}) async-start(), calls=%async_computation.2 | async-start | bytes 3538944 | tf_op jit(solution)/shard_map/all_gather | solution.py:111
  26.5 1.1 copy-start.1
  64.9 0.7 copy-start.4
  65.7 8.4 %collective-permute-start = (bf16[256,256]{1,0:T(8,128)(2,1)S(1)}, bf16[256,256]{1,0:T(8,128)(2,1)S(1)}, u32[]{:S(2)}, u32[]{:S(2)}) collective-permute-start(bf16[256,256]{1,0:T(8,128)(2,1)S(1)} %get-tuple-element.34), channel_id=1, source_target_pairs={{0,1},{1,2},{2,3},{3,4},{4,5},{5,6},{6,7},{7,8},{8,9},{9,10},{10,1... | collective-permute-start | bytes 393224 | tf_op jit(solution)/shard_map/ppermute | solution.py:16
  66.4 7.7 %collective-permute-start.1 = (bf16[256,256]{1,0:T(8,128)(2,1)S(1)}, bf16[256,256]{1,0:T(8,128)(2,1)S(1)}, u32[]{:S(2)}, u32[]{:S(2)}) collective-permute-start(bf16[256,256]{1,0:T(8,128)(2,1)S(1)} %get-tuple-element.35), channel_id=1, source_target_pairs={{1,0},{2,1},{3,2},{4,3},{5,4},{6,5},{7,6},{8,7},{9,8},{10,9},{11,1... | collective-permute-start | bytes 393224 | tf_op jit(solution)/shard_map/ppermute | solution.py:18
  75.1 2.6 %copy-start.2 = (bf16[6,8,128,128]{3,2,1,0:T(8,128)(2,1)S(1)}, bf16[6,8,128,128]{3,2,1,0:T(8,128)(2,1)}, u32[]{:S(2)}) copy-start(bf16[6,8,128,128]{3,2,1,0:T(8,128)(2,1)} %copy-done.1) | copy-start | bytes 4718596
  75.1 2.6 %copy-start.5 = (bf16[768,256]{1,0:T(8,128)(2,1)S(1)}, bf16[768,256]{1,0:T(8,128)(2,1)}, u32[]{:S(2)}) copy-start(bf16[768,256]{1,0:T(8,128)(2,1)} %copy-done.4) | copy-start | bytes 1179652
  75.1 2.6 %copy-start.10 = (f32[256]{0:T(256)S(1)}, f32[256]{0:T(256)}, u32[]{:S(2)}) copy-start(f32[256]{0:T(256)} %param.13) | copy-start | bytes 3076
  77.7 2.8 %copy-start.3 = (bf16[10,6,128,128]{3,0,2,1:T(8,128)(2,1)S(1)}, bf16[10,6,128,128]{3,0,2,1:T(8,128)(2,1)}, u32[]{:S(2)}) copy-start(bf16[10,6,128,128]{3,0,2,1:T(8,128)(2,1)} %convert_bitcast_fusion) | copy-start | bytes 5898244
  77.7 2.9 %copy-start.7 = (bf16[768,256]{1,0:T(8,128)(2,1)S(1)}, bf16[768,256]{1,0:T(8,128)(2,1)}, u32[]{:S(2)}) copy-start(bf16[768,256]{1,0:T(8,128)(2,1)} %param.17) | copy-start | bytes 1179652
  82.1 8.4 %collective-permute-start.2 = (bf16[2,128,256]{2,1,0:T(8,128)(2,1)S(1)}, bf16[2,128,256]{2,1,0:T(8,128)(2,1)S(1)}, u32[]{:S(2)}, u32[]{:S(2)}) collective-permute-start(bf16[2,128,256]{2,1,0:T(8,128)(2,1)S(1)} %get-tuple-element.33), channel_id=1, source_target_pairs={{15,0},{0,1},{1,2},{2,3},{3,4},{4,5},{5,6},{6,7},{7,8},{8,9},{9,10... | collective-permute-start | bytes 393224 | tf_op jit(solution)/shard_map/ppermute | solution.py:28
  82.2 50.6 %copy-start.6 = (bf16[16,128,48]{1,2,0:T(8,128)(2,1)S(1)}, bf16[16,128,48]{1,2,0:T(8,128)(2,1)}, u32[]{:S(2)}) copy-start(bf16[16,128,48]{1,2,0:T(8,128)(2,1)} %param.11) | copy-start | bytes 589828
  83.6 7.9 %collective-permute-start.3 = (bf16[2,128,256]{2,1,0:T(8,128)(2,1)S(1)}, bf16[2,128,256]{2,1,0:T(8,128)(2,1)S(1)}, u32[]{:S(2)}, u32[]{:S(2)}) collective-permute-start(bf16[2,128,256]{2,1,0:T(8,128)(2,1)S(1)} %get-tuple-element.32), channel_id=1, source_target_pairs={{1,0},{2,1},{3,2},{4,3},{5,4},{6,5},{7,6},{8,7},{9,8},{10,9},{11,1... | collective-permute-start | bytes 393224 | tf_op jit(solution)/shard_map/ppermute | solution.py:28
Sparse Core Ops, SparseCore 0:
  108.9 23.8 all-gather.1
where the time goes:
time: 217 us
  blocking collectives  90.9 us (42%)
  waiting for transfers between devices  63.2 us (29%)
  starting transfers between devices  22 us (10%)
  between operations  14.2 us (7%)
  matrix products  11.6 us (5%)
  local copies, waits for them, and re-layouts  9.55 us (4%)
  other arithmetic  5.11 us (2%)
    psum x1, blocking collectives, body(): weight_grad = lax.psum(grad_slice, 'rows')  74.5 us
    all_to_all x1, waiting for transfers between devices, body(): lax.all_to_all(partial_value, ('feat', 'rows'), split_axis=0, concat_axis...  33.8 us
    all_gather x1, waiting for transfers between devices, body(): lax.all_gather(pieces, 'feat', axis=0, tiled=True)  24 us
    all_to_all x1, blocking collectives, body(): lax.all_to_all(grad_proj.reshape(row_size, sub_rows, hidden_width), 'rows...  16.3 us
    all_to_all x1, starting transfers between devices, body(): lax.all_to_all(partial_value, ('feat', 'rows'), split_axis=0, concat_axis...  11.1 us
    ppermute x2, starting transfers between devices, shifted(): return lax.ppermute(block, axis, route)  5.42 us
    ppermute x1, starting transfers between devices, padded(): lax.ppermute(head, axis, [((i + 1) % count, i) for i in range(count)])  4.74 us
  transfers between devices with their start and end apart: 6, of which 5 were waited for; matrix products, arithmetic and copies ran while one was open for 3% of the time, Pallas kernels for 0%

commit v1 on v0

--- a/solution.py
+++ b/solution.py
@@ -4,6 +4,20 @@
 from jax.sharding import PartitionSpec as P
 
 HALO_BLK = 2
+
+
+def arrange_field(array_in, a_name, row_data):
+    built, x_now = (jax.lax.psum(1, a_name), jax.lax.axis_index(a_name))
+    samples = [(hop_no, (hop_no - 1) % built) for hop_no in range(built)]
+    value_now = array_in.shape[0]
+    b_next = array_in
+    h_now = row_data(b_next, x_now * value_now)
+    idx = 1
+    while idx < built:
+        b_next = jax.lax.ppermute(b_next, a_name, samples)
+        h_now = h_now + row_data(b_next, (x_now + idx) % built * value_now)
+        idx = idx + 1
+    return h_now
 
 
 def padded(cells, sides, width):
@@ -105,11 +119,15 @@
         concat_axis=0,
         tiled=True,
     )
-    grad_slice = jnp.einsum(
-        "cdn,dnh->ch",
-        features,
-        lax.all_gather(pieces, "feat", axis=0, tiled=True),
-        preferred_element_type=jnp.float32,
+    grad_slice = arrange_field(
+        pieces,
+        "feat",
+        lambda shard, start: jnp.einsum(
+            "cdn,dnh->ch",
+            lax.dynamic_slice_in_dim(features, start, shard.shape[0], axis=1),
+            shard,
+            preferred_element_type=jnp.float32,
+        ),
     )
     weight_grad = lax.psum(grad_slice, "rows")
     return (hidden, weight_grad)

time: 217 us -> 228 us (1.051)
  starting transfers between devices: 22 us -> 40.7 us
  between operations: 14.2 us -> 0.92 us
  waiting for transfers between devices: 63.2 us -> 71.7 us
  blocking collectives: 90.9 us -> 86.9 us
    ppermute x0 -> x7, waiting for transfers between devices: none -> 32.4 us  [arrange_field(): b_next = jax.lax.ppermute(b_next, a_name, samples)]
    all_gather x1 -> x0, waiting for transfers between devices: 24 us -> none  [body(): lax.all_gather(pieces, 'feat', axis=0, tiled=True)]
    ppermute x0 -> x7, starting transfers between devices: none -> 18.7 us  [arrange_field(): b_next = jax.lax.ppermute(b_next, a_name, samples)]
    psum x1, blocking collectives: 74.5 us -> 70.6 us  [body(): weight_grad = lax.psum(grad_slice, 'rows')]
    unnamed x22 -> x34, local copies, waits for them, and re-layouts: 2.84 us -> 4.56 us
  transfers between devices with their start and end apart: 6 -> 12, of which waited for: 5 -> 11; matrix products, arithmetic and copies ran while one was open for 3% -> 5% of each run, Pallas kernels for 0% -> 0%
where the time goes in v1:
time: 228 us
  blocking collectives  86.9 us (38%)
  waiting for transfers between devices  71.7 us (31%)
  starting transfers between devices  40.7 us (18%)
  matrix products  11.7 us (5%)
  local copies, waits for them, and re-layouts  10.9 us (5%)
  other arithmetic  5.11 us (2%)
    psum x1, blocking collectives, body(): weight_grad = lax.psum(grad_slice, 'rows')  70.6 us
    all_to_all x1, waiting for transfers between devices, body(): lax.all_to_all(partial_value, ('feat', 'rows'), split_axis=0, concat_axis...  33.9 us
    ppermute x7, waiting for transfers between devices, arrange_field(): b_next = jax.lax.ppermute(b_next, a_name, samples)  32.4 us
    ppermute x7, starting transfers between devices, arrange_field(): b_next = jax.lax.ppermute(b_next, a_name, samples)  18.7 us
    all_to_all x1, blocking collectives, body(): lax.all_to_all(grad_proj.reshape(row_size, sub_rows, hidden_width), 'rows...  16.3 us
    all_to_all x1, starting transfers between devices, body(): lax.all_to_all(partial_value, ('feat', 'rows'), split_axis=0, concat_axis...  11.1 us
    ppermute x2, starting transfers between devices, shifted(): return lax.ppermute(block, axis, route)  5.42 us
    ppermute x1, starting transfers between devices, padded(): lax.ppermute(head, axis, [((i + 1) % count, i) for i in range(count)])  4.74 us
  transfers between devices with their start and end apart: 12, of which 11 were waited for; matrix products, arithmetic and copies ran while one was open for 5% of the time, Pallas kernels for 0%

profile of v1, /device:TPU:0, one launch (start us, length us, event | category | flops | bytes accessed | tf_op | source)
XLA Modules:
  0.0 227.9 jit_solution(1332541207921715408)
XLA Ops:
  0.6 0.0 copy-start
  0.7 0.8 copy-done
  1.5 1.9 convert_bitcast_fusion.1
  3.4 3.2 %copy.29 = bf16[128,48,256]{2,1,0:T(8,128)(2,1)} copy(bf16[128,48,256]{0,2,1:T(8,128)(2,1)S(1)} %convert_bitcast_fusion.1) | data formatting | bytes 6291456 | tf_op jit(solution)/shard_map/convert_element_type | solution.py:73
  6.6 11.1 %all-to-all-start = ((bf16[128,48,256]{2,1,0:T(8,128)(2,1)}), bf16[128,48,256]{2,1,0:T(8,128)(2,1)S(1)}, u32[]{:S(2)}, u32[]{:S(2)}) async-start(bf16[128,48,256]{2,1,0:T(8,128)(2,1)} %copy.29), calls=%async_computation | async-start | bytes 6291456 | tf_op jit(solution)/shard_map/all_to_all | solution.py:74
  17.8 0.1 fusion.33
  17.9 2.0 convert_reduce_fusion
  19.9 1.1 copy-done.2
  21.1 3.1 %convert_bitcast_fusion = bf16[10,6,128,128]{3,0,2,1:T(8,128)(2,1)} fusion(bf16[6,8,128,128]{3,2,1,0:T(8,128)(2,1)S(1)} %get-tuple-element.27, s32[6,8]{1,0:T(8,128)S(1)} %get-tuple-element.29), kind=kOutput, calls=%fused_computation.2 | convolution fusion | flops 16712160 | bytes 3539136 | tf_op jit(solution)/shard_map/bkq,bkij->qbij/dot_general | solution.py:103
  24.1 33.9 %all-to-all-done = bf16[128,48,256]{2,1,0:T(8,128)(2,1)S(1)} async-done(((bf16[128,48,256]{2,1,0:T(8,128)(2,1)}), bf16[128,48,256]{2,1,0:T(8,128)(2,1)S(1)}, u32[]{:S(2)}, u32[]{:S(2)}) %all-to-all-start) | async-done | bytes 3145760 | tf_op jit(solution)/shard_map/all_to_all | solution.py:74
  58.0 0.4 bitcast_reduce_fusion
  58.4 0.0 copy-start.5
  58.5 0.7 copy-done.5
  59.2 0.7 collective-permute-start
  59.9 4.7 %collective-permute-start.1 = (bf16[256,256]{1,0:T(8,128)(2,1)S(1)}, bf16[256,256]{1,0:T(8,128)(2,1)S(1)}, u32[]{:S(2)}, u32[]{:S(2)}) collective-permute-start(bf16[256,256]{1,0:T(8,128)(2,1)S(1)} %get-tuple-element.35), channel_id=1, source_target_pairs={{1,0},{2,1},{3,2},{4,3},{5,4},{6,5},{7,6},{8,7},{9,8},{10,9},{11,1... | collective-permute-start | bytes 393224 | tf_op jit(solution)/shard_map/ppermute | solution.py:32
  64.6 0.1 reshape.114
  64.7 2.9 %collective-permute-done = bf16[256,256]{1,0:T(8,128)(2,1)S(1)} collective-permute-done((bf16[256,256]{1,0:T(8,128)(2,1)S(1)}, bf16[256,256]{1,0:T(8,128)(2,1)S(1)}, u32[]{:S(2)}, u32[]{:S(2)}) %collective-permute-start) | collective-permute-done | bytes 131104 | tf_op jit(solution)/shard_map/ppermute | solution.py:30
  67.6 1.0 pad_maximum_fusion
  68.6 2.5 %gather_fusion = bf16[48,128,256]{2,1,0:T(8,128)(2,1)} fusion(bf16[10,128,256]{2,1,0:T(8,128)(2,1)S(1)} %bitcast.88, s32[1024]{0:T(1024)S(1)} %pad_clamp_fusion), kind=kCustom, calls=%fused_computation | custom fusion | bytes 6291648 | tf_op jit(solution)/shard_map/gather | solution.py:88
  71.2 0.0 copy-start.7
  71.2 2.8 %fusion.8 = f32[6,128,256]{2,1,0:T(8,128)S(1)} fusion(bf16[6,8,128,128]{3,2,1,0:T(8,128)(2,1)S(1)} %copy-done.3, bf16[6,8,128,256]{3,2,1,0:T(8,128)(2,1)} %bitcast.90, bf16[6,128,256]{2,1,0:T(8,128)(2,1)S(1)} %bitcast.91, f32[256]{0:T(256)S(1)} %copy-done.12, f32[6,128]{1,0:T(8,128)S(1)} %broadcast_add_fusion), kind=kOutput, calls=%fused_computation.12 | convolution fusion | flops 403439616 | bytes 5902336 | tf_op jit(solution)/shard_map/bkij,bkjh->bih/dot_general | solution.py:89
  74.0 0.0 copy-done.4
  74.0 0.1 copy-done.7
  74.1 1.5 fusion.38
  75.6 0.1 collective-permute-start.2
  75.7 1.4 slice_add_fusion
  77.1 5.3 %collective-permute-start.3 = (bf16[2,128,256]{2,1,0:T(8,128)(2,1)S(1)}, bf16[2,128,256]{2,1,0:T(8,128)(2,1)S(1)}, u32[]{:S(2)}, u32[]{:S(2)}) collective-permute-start(bf16[2,128,256]{2,1,0:T(8,128)(2,1)S(1)} %get-tuple-element.32), channel_id=1, source_target_pairs={{1,0},{2,1},{3,2},{4,3},{5,4},{6,5},{7,6},{8,7},{9,8},{10,9},{11,1... | collective-permute-start | bytes 393224 | tf_op jit(solution)/shard_map/ppermute | solution.py:42
  82.4 1.6 collective-permute-done.2
  84.0 0.1 fusion.26
  84.0 0.9 collective-permute-done.3
  84.9 0.1 fusion.25
  85.0 16.3 %all_to_all.10 = bf16[16,48,256]{2,1,0:T(8,128)(2,1)S(1)} all-to-all(bf16[16,48,256]{2,1,0:T(8,128)(2,1)S(1)} %bitcast.92), channel_id=1, replica_groups=mesh['feat'=8,'rows'=16] {'rows'}, dimensions={0} | all-to-all | bytes 786432 | tf_op jit(solution)/shard_map/all_to_all | solution.py:115
  101.4 5.3 %collective-permute-done.4 = bf16[16,48,256]{2,1,0:T(8,128)(2,1)S(1)} collective-permute-done((bf16[16,48,256]{2,1,0:T(8,128)(2,1)S(1)}, bf16[16,48,256]{2,1,0:T(8,128)(2,1)S(1)}, u32[]{:S(2)}, u32[]{:S(2)}) %collective-permute-start.4) | collective-permute-done | bytes 393248 | tf_op jit(solution)/shard_map/ppermute | solution.py:17
  106.7 3.1 %collective-permute-start.5 = (bf16[16,48,256]{2,1,0:T(8,128)(2,1)S(1)}, bf16[16,48,256]{2,1,0:T(8,128)(2,1)S(1)}, u32[]{:S(2)}, u32[]{:S(2)}) collective-permute-start(bf16[16,48,256]{2,1,0:T(8,128)(2,1)S(1)} %collective-permute-done.4), channel_id=1, source_target_pairs={{0,112},{16,0},{32,16},{48,32},{64,48},{80,64},{96,80},{112,96},{1... | collective-permute-start | bytes 1179656 | tf_op jit(solution)/shard_map/ppermute | solution.py:17
  109.8 5.3 %collective-permute-done.5 = bf16[16,48,256]{2,1,0:T(8,128)(2,1)S(1)} collective-permute-done((bf16[16,48,256]{2,1,0:T(8,128)(2,1)S(1)}, bf16[16,48,256]{2,1,0:T(8,128)(2,1)S(1)}, u32[]{:S(2)}, u32[]{:S(2)}) %collective-permute-start.5) | collective-permute-done | bytes 393248 | tf_op jit(solution)/shard_map/ppermute | solution.py:17
  115.1 3.1 %collective-permute-start.6 = (bf16[16,48,256]{2,1,0:T(8,128)(2,1)S(1)}, bf16[16,48,256]{2,1,0:T(8,128)(2,1)S(1)}, u32[]{:S(2)}, u32[]{:S(2)}) collective-permute-start(bf16[16,48,256]{2,1,0:T(8,128)(2,1)S(1)} %collective-permute-done.5), channel_id=1, source_target_pairs={{0,112},{16,0},{32,16},{48,32},{64,48},{80,64},{96,80},{112,96},{1... | collective-permute-start | bytes 1179656 | tf_op jit(solution)/shard_map/ppermute | solution.py:17
  118.2 5.3 %collective-permute-done.6 = bf16[16,48,256]{2,1,0:T(8,128)(2,1)S(1)} collective-permute-done((bf16[16,48,256]{2,1,0:T(8,128)(2,1)S(1)}, bf16[16,48,256]{2,1,0:T(8,128)(2,1)S(1)}, u32[]{:S(2)}, u32[]{:S(2)}) %collective-permute-start.6) | collective-permute-done | bytes 393248 | tf_op jit(solution)/shard_map/ppermute | solution.py:17
  123.5 3.1 %collective-permute-start.7 = (bf16[16,48,256]{2,1,0:T(8,128)(2,1)S(1)}, bf16[16,48,256]{2,1,0:T(8,128)(2,1)S(1)}, u32[]{:S(2)}, u32[]{:S(2)}) collective-permute-start(bf16[16,48,256]{2,1,0:T(8,128)(2,1)S(1)} %collective-permute-done.6), channel_id=1, source_target_pairs={{0,112},{16,0},{32,16},{48,32},{64,48},{80,64},{96,80},{112,96},{1... | collective-permute-start | bytes 1179656 | tf_op jit(solution)/shard_map/ppermute | solution.py:17
  126.6 0.5 constant_dynamic-slice_fusion
  127.2 0.8 copy.43
  127.9 0.1 copy.44
  128.1 0.1 copy.45
  128.2 0.1 copy.46
  128.3 0.1 copy.47
  128.5 0.1 copy.48
  128.6 0.1 copy.49
  128.8 0.1 copy.50
  128.9 1.0 convolution_bitcast_fusion.8
  130.0 2.0 collective-permute-done.7
  131.9 3.1 %collective-permute-start.8 = (bf16[16,48,256]{2,1,0:T(8,128)(2,1)S(1)}, bf16[16,48,256]{2,1,0:T(8,128)(2,1)S(1)}, u32[]{:S(2)}, u32[]{:S(2)}) collective-permute-start(bf16[16,48,256]{2,1,0:T(8,128)(2,1)S(1)} %collective-permute-done.7), channel_id=1, source_target_pairs={{0,112},{16,0},{32,16},{48,32},{64,48},{80,64},{96,80},{112,96},{1... | collective-permute-start | bytes 1179656 | tf_op jit(solution)/shard_map/ppermute | solution.py:17
  135.0 0.2 fusion.15
  135.2 0.0 copy-done.9
  135.2 0.2 fusion.14
  135.5 4.9 %collective-permute-done.8 = bf16[16,48,256]{2,1,0:T(8,128)(2,1)S(1)} collective-permute-done((bf16[16,48,256]{2,1,0:T(8,128)(2,1)S(1)}, bf16[16,48,256]{2,1,0:T(8,128)(2,1)S(1)}, u32[]{:S(2)}, u32[]{:S(2)}) %collective-permute-start.8) | collective-permute-done | bytes 393248 | tf_op jit(solution)/shard_map/ppermute | solution.py:17
  140.3 3.1 %collective-permute-start.9 = (bf16[16,48,256]{2,1,0:T(8,128)(2,1)S(1)}, bf16[16,48,256]{2,1,0:T(8,128)(2,1)S(1)}, u32[]{:S(2)}, u32[]{:S(2)}) collective-permute-start(bf16[16,48,256]{2,1,0:T(8,128)(2,1)S(1)} %collective-permute-done.8), channel_id=1, source_target_pairs={{0,112},{16,0},{32,16},{48,32},{64,48},{80,64},{96,80},{112,96},{1... | collective-permute-start | bytes 1179656 | tf_op jit(solution)/shard_map/ppermute | solution.py:17
  143.4 0.2 fusion.13
  143.6 0.2 fusion.12
  143.9 4.9 %collective-permute-done.9 = bf16[16,48,256]{2,1,0:T(8,128)(2,1)S(1)} collective-permute-done((bf16[16,48,256]{2,1,0:T(8,128)(2,1)S(1)}, bf16[16,48,256]{2,1,0:T(8,128)(2,1)S(1)}, u32[]{:S(2)}, u32[]{:S(2)}) %collective-permute-start.9) | collective-permute-done | bytes 393248 | tf_op jit(solution)/shard_map/ppermute | solution.py:17
  148.7 3.1 %collective-permute-start.10 = (bf16[16,48,256]{2,1,0:T(8,128)(2,1)S(1)}, bf16[16,48,256]{2,1,0:T(8,128)(2,1)S(1)}, u32[]{:S(2)}, u32[]{:S(2)}) collective-permute-start(bf16[16,48,256]{2,1,0:T(8,128)(2,1)S(1)} %collective-permute-done.9), channel_id=1, source_target_pairs={{0,112},{16,0},{32,16},{48,32},{64,48},{80,64},{96,80},{112,96},{1... | collective-permute-start | bytes 1179656 | tf_op jit(solution)/shard_map/ppermute | solution.py:17
  151.9 0.2 fusion.11
  152.1 0.2 fusion.10
  152.3 4.9 %collective-permute-done.10 = bf16[16,48,256]{2,1,0:T(8,128)(2,1)S(1)} collective-permute-done((bf16[16,48,256]{2,1,0:T(8,128)(2,1)S(1)}, bf16[16,48,256]{2,1,0:T(8,128)(2,1)S(1)}, u32[]{:S(2)}, u32[]{:S(2)}) %collective-permute-start.10) | collective-permute-done | bytes 393248 | tf_op jit(solution)/shard_map/ppermute | solution.py:17
  157.2 0.2 fusion.9
  157.4 70.6 %psum.7 = f32[16,256]{1,0:T(8,128)} all-reduce(f32[16,256]{1,0:T(8,128)S(1)} %fusion.9), channel_id=1, replica_groups=mesh['feat'=8,'rows'=16] {'rows'}, use_global_device_ids=true, to_apply=%region_2.3 | all-reduce | flops 4096 | bytes 32768 | tf_op jit(solution)/shard_map/psum | solution.py:132
  (25 shorter events, 0.1 us)
Async XLA Ops:
  0.6 0.8 copy-start
  6.6 11.2 %copy-start.11 = (s32[6]{0:T(128)S(1)}, s32[6]{0:T(128)}, u32[]{:S(2)}) copy-start(s32[6]{0:T(128)} %param.16) | copy-start | bytes 76
  6.6 11.2 %copy-start.10 = (s32[6,8]{1,0:T(8,128)S(1)}, s32[6,8]{1,0:T(8,128)}, u32[]{:S(2)}) copy-start(s32[6,8]{1,0:T(8,128)} %param.15) | copy-start | bytes 580
  6.6 51.4 %all-to-all-start = ((bf16[128,48,256]{2,1,0:T(8,128)(2,1)}), bf16[128,48,256]{2,1,0:T(8,128)(2,1)S(1)}, u32[]{:S(2)}, u32[]{:S(2)}) async-start(bf16[128,48,256]{2,1,0:T(8,128)(2,1)} %copy.29), calls=%async_computation | async-start | bytes 6291456 | tf_op jit(solution)/shard_map/all_to_all | solution.py:74
  19.9 1.1 copy-start.2
  58.4 0.7 copy-start.5
  59.2 8.4 %collective-permute-start = (bf16[256,256]{1,0:T(8,128)(2,1)S(1)}, bf16[256,256]{1,0:T(8,128)(2,1)S(1)}, u32[]{:S(2)}, u32[]{:S(2)}) collective-permute-start(bf16[256,256]{1,0:T(8,128)(2,1)S(1)} %get-tuple-element.34), channel_id=1, source_target_pairs={{0,1},{1,2},{2,3},{3,4},{4,5},{5,6},{6,7},{7,8},{8,9},{9,10},{10,1... | collective-permute-start | bytes 393224 | tf_op jit(solution)/shard_map/ppermute | solution.py:30
  59.9 7.7 %collective-permute-start.1 = (bf16[256,256]{1,0:T(8,128)(2,1)S(1)}, bf16[256,256]{1,0:T(8,128)(2,1)S(1)}, u32[]{:S(2)}, u32[]{:S(2)}) collective-permute-start(bf16[256,256]{1,0:T(8,128)(2,1)S(1)} %get-tuple-element.35), channel_id=1, source_target_pairs={{1,0},{2,1},{3,2},{4,3},{5,4},{6,5},{7,6},{8,7},{9,8},{10,9},{11,1... | collective-permute-start | bytes 393224 | tf_op jit(solution)/shard_map/ppermute | solution.py:32
  68.6 2.6 %copy-start.3 = (bf16[6,8,128,128]{3,2,1,0:T(8,128)(2,1)S(1)}, bf16[6,8,128,128]{3,2,1,0:T(8,128)(2,1)}, u32[]{:S(2)}) copy-start(bf16[6,8,128,128]{3,2,1,0:T(8,128)(2,1)} %copy-done.2) | copy-start | bytes 4718596
  68.6 2.6 %copy-start.6 = (bf16[768,256]{1,0:T(8,128)(2,1)S(1)}, bf16[768,256]{1,0:T(8,128)(2,1)}, u32[]{:S(2)}) copy-start(bf16[768,256]{1,0:T(8,128)(2,1)} %copy-done.5) | copy-start | bytes 1179652
  68.6 2.6 %copy-start.12 = (f32[256]{0:T(256)S(1)}, f32[256]{0:T(256)}, u32[]{:S(2)}) copy-start(f32[256]{0:T(256)} %param.13) | copy-start | bytes 3076
  71.2 2.8 %copy-start.4 = (bf16[10,6,128,128]{3,0,2,1:T(8,128)(2,1)S(1)}, bf16[10,6,128,128]{3,0,2,1:T(8,128)(2,1)}, u32[]{:S(2)}) copy-start(bf16[10,6,128,128]{3,0,2,1:T(8,128)(2,1)} %convert_bitcast_fusion) | copy-start | bytes 5898244
  71.2 2.9 %copy-start.7 = (bf16[768,256]{1,0:T(8,128)(2,1)S(1)}, bf16[768,256]{1,0:T(8,128)(2,1)}, u32[]{:S(2)}) copy-start(bf16[768,256]{1,0:T(8,128)(2,1)} %param.17) | copy-start | bytes 1179652
  75.6 8.4 %collective-permute-start.2 = (bf16[2,128,256]{2,1,0:T(8,128)(2,1)S(1)}, bf16[2,128,256]{2,1,0:T(8,128)(2,1)S(1)}, u32[]{:S(2)}, u32[]{:S(2)}) collective-permute-start(bf16[2,128,256]{2,1,0:T(8,128)(2,1)S(1)} %get-tuple-element.33), channel_id=1, source_target_pairs={{15,0},{0,1},{1,2},{2,3},{3,4},{4,5},{5,6},{6,7},{7,8},{8,9},{9,10... | collective-permute-start | bytes 393224 | tf_op jit(solution)/shard_map/ppermute | solution.py:42
  77.1 49.6 %copy-start.1 = (bf16[16,128,48]{1,2,0:T(8,128)(2,1)S(1)}, bf16[16,128,48]{1,2,0:T(8,128)(2,1)}, u32[]{:S(2)}) copy-start(bf16[16,128,48]{1,2,0:T(8,128)(2,1)} %param.11) | copy-start | bytes 589828
  77.1 7.9 %collective-permute-start.3 = (bf16[2,128,256]{2,1,0:T(8,128)(2,1)S(1)}, bf16[2,128,256]{2,1,0:T(8,128)(2,1)S(1)}, u32[]{:S(2)}, u32[]{:S(2)}) collective-permute-start(bf16[2,128,256]{2,1,0:T(8,128)(2,1)S(1)} %get-tuple-element.32), channel_id=1, source_target_pairs={{1,0},{2,1},{3,2},{4,3},{5,4},{6,5},{7,6},{8,7},{9,8},{10,9},{11,1... | collective-permute-start | bytes 393224 | tf_op jit(solution)/shard_map/ppermute | solution.py:42
  101.4 5.3 %collective-permute-start.4 = (bf16[16,48,256]{2,1,0:T(8,128)(2,1)S(1)}, bf16[16,48,256]{2,1,0:T(8,128)(2,1)S(1)}, u32[]{:S(2)}, u32[]{:S(2)}) collective-permute-start(bf16[16,48,256]{2,1,0:T(8,128)(2,1)S(1)} %all_to_all.10), channel_id=1, source_target_pairs={{0,112},{16,0},{32,16},{48,32},{64,48},{80,64},{96,80},{112,96},{1... | collective-permute-start | bytes 1179656 | tf_op jit(solution)/shard_map/ppermute | solution.py:17
  106.7 8.4 %collective-permute-start.5 = (bf16[16,48,256]{2,1,0:T(8,128)(2,1)S(1)}, bf16[16,48,256]{2,1,0:T(8,128)(2,1)S(1)}, u32[]{:S(2)}, u32[]{:S(2)}) collective-permute-start(bf16[16,48,256]{2,1,0:T(8,128)(2,1)S(1)} %collective-permute-done.4), channel_id=1, source_target_pairs={{0,112},{16,0},{32,16},{48,32},{64,48},{80,64},{96,80},{112,96},{1... | collective-permute-start | bytes 1179656 | tf_op jit(solution)/shard_map/ppermute | solution.py:17
  115.1 11.5 %copy-start.8 = (bf16[16,48,256]{2,1,0:T(8,128)(2,1)}, bf16[16,48,256]{2,1,0:T(8,128)(2,1)S(1)}, u32[]{:S(2)}) copy-start(bf16[16,48,256]{2,1,0:T(8,128)(2,1)S(1)} %collective-permute-done.5) | copy-start | bytes 1179652
  115.1 8.4 %collective-permute-start.6 = (bf16[16,48,256]{2,1,0:T(8,128)(2,1)S(1)}, bf16[16,48,256]{2,1,0:T(8,128)(2,1)S(1)}, u32[]{:S(2)}, u32[]{:S(2)}) collective-permute-start(bf16[16,48,256]{2,1,0:T(8,128)(2,1)S(1)} %collective-permute-done.5), channel_id=1, source_target_pairs={{0,112},{16,0},{32,16},{48,32},{64,48},{80,64},{96,80},{112,96},{1... | collective-permute-start | bytes 1179656 | tf_op jit(solution)/shard_map/ppermute | solution.py:17
  123.5 8.4 %collective-permute-start.7 = (bf16[16,48,256]{2,1,0:T(8,128)(2,1)S(1)}, bf16[16,48,256]{2,1,0:T(8,128)(2,1)S(1)}, u32[]{:S(2)}, u32[]{:S(2)}) collective-permute-start(bf16[16,48,256]{2,1,0:T(8,128)(2,1)S(1)} %collective-permute-done.6), channel_id=1, source_target_pairs={{0,112},{16,0},{32,16},{48,32},{64,48},{80,64},{96,80},{112,96},{1... | collective-permute-start | bytes 1179656 | tf_op jit(solution)/shard_map/ppermute | solution.py:17
  128.1 7.2 %copy-start.9 = (bf16[16,48,256]{2,1,0:T(8,128)(2,1)S(1)}, bf16[16,48,256]{2,1,0:T(8,128)(2,1)}, u32[]{:S(2)}) copy-start(bf16[16,48,256]{2,1,0:T(8,128)(2,1)} %copy-done.8) | copy-start | bytes 1179652
  131.9 8.4 %collective-permute-start.8 = (bf16[16,48,256]{2,1,0:T(8,128)(2,1)S(1)}, bf16[16,48,256]{2,1,0:T(8,128)(2,1)S(1)}, u32[]{:S(2)}, u32[]{:S(2)}) collective-permute-start(bf16[16,48,256]{2,1,0:T(8,128)(2,1)S(1)} %collective-permute-done.7), channel_id=1, source_target_pairs={{0,112},{16,0},{32,16},{48,32},{64,48},{80,64},{96,80},{112,96},{1... | collective-permute-start | bytes 1179656 | tf_op jit(solution)/shard_map/ppermute | solution.py:17
  140.3 8.4 %collective-permute-start.9 = (bf16[16,48,256]{2,1,0:T(8,128)(2,1)S(1)}, bf16[16,48,256]{2,1,0:T(8,128)(2,1)S(1)}, u32[]{:S(2)}, u32[]{:S(2)}) collective-permute-start(bf16[16,48,256]{2,1,0:T(8,128)(2,1)S(1)} %collective-permute-done.8), channel_id=1, source_target_pairs={{0,112},{16,0},{32,16},{48,32},{64,48},{80,64},{96,80},{112,96},{1... | collective-permute-start | bytes 1179656 | tf_op jit(solution)/shard_map/ppermute | solution.py:17
  148.7 8.4 %collective-permute-start.10 = (bf16[16,48,256]{2,1,0:T(8,128)(2,1)S(1)}, bf16[16,48,256]{2,1,0:T(8,128)(2,1)S(1)}, u32[]{:S(2)}, u32[]{:S(2)}) collective-permute-start(bf16[16,48,256]{2,1,0:T(8,128)(2,1)S(1)} %collective-permute-done.9), channel_id=1, source_target_pairs={{0,112},{16,0},{32,16},{48,32},{64,48},{80,64},{96,80},{112,96},{1... | collective-permute-start | bytes 1179656 | tf_op jit(solution)/shard_map/ppermute | solution.py:17
